TPU v7x, 32 devices: a whole 2x2x4 slice. The times are simulated.
32 devices in a mesh: rep: 2 (over y), seq: 4 (over z), tp: 2 (over x), pp: 2 (over core).
Axes of the slice: x: 2, y: 2, z: 4, core: 2. Of those that a mesh axis runs over, the one named last changes fastest.
Arguments:
- queries: bfloat16 [128, 32, 8192], P(('rep', 'seq'), None, ('tp', 'pp')), parts along dimension 0, may hold values from -26 to 26
- resp_kv: bfloat16 [128, 32, 8, 256], P(('rep', 'seq'), None, 'tp'), parts along dimension 0, may hold values from -4.5 to 4.5
- prompt_kv: bfloat16 [8, 2048, 8, 256], P(('rep', 'seq'), None, 'tp'), parts along dimension 0, may hold values from -4.5 to 4.5
- lengths: int32 [128], P(('rep', 'seq')), parts along dimension 0, may hold values from 8 to 32
- group_of: int32 [128], P(('rep', 'seq')), parts along dimension 0, may hold values from 0 to 3, as said below
Outputs:
- mixed: bfloat16 [128, 32, 8192], P(('rep', 'seq'), None, ('tp', 'pp')), parts along dimension 0
There are 2 independent parts, one for each index of `rep`. A program takes and returns all parts, laid end to end along the dimension named above; each array names one. Nothing has to cross between parts.
Inputs may be any that keep to these rules, and one draw needn't show every extreme that they name: `group_of`: each device of seq holds 16 responses; every prompt is answered by exactly 16 responses; at most 8 of the responses of one device answer the same prompt, and every device has a prompt with exactly 8 of its responses.
All inputs are finite; a program needn't handle non-finite values.
Results may differ from a plain program's by a relative error of at most 0.0049.
Values may be sent and summed in bfloat16 or wider, within the bound.
No kernel may reach another device: no remote copies, remote signals or barrier semaphores. Data moves between devices by JAX's collectives and lax.ppermute only.
A program may use at most 128 MiB of HBM per device.

v0:
```python
import functools
import math

import jax
import jax.numpy as jnp
from jax import lax
from jax.experimental import pallas as pl
from jax.experimental.pallas import tpu as pltpu
from jax.sharding import PartitionSpec as P

QHEADS = 64
KVH = 8
HD = 128
LOG2E = math.log2(math.e)
VMEM_BYTES = 12 * 1024 * 1024
SLOTS = 8
HBM = pl.BlockSpec(memory_space=pl.ANY)
SMEM = pl.BlockSpec(memory_space=pltpu.SMEM)
VMEM = pl.BlockSpec(memory_space=pltpu.VMEM)


TN = (((0,), (0,)), ((), ()))
BLOCK = 512
SCORE_BLOCK = 1024
CHUNK = 32
GROUPS = 12


def stacked_heads(q_tile, per_kv):
    return jnp.concatenate([q_tile[:, g * HD:(g + 1) * HD] for g in range(per_kv)], axis=0)


def own_scores(own_tile, q_cols, rlen):
    own = jnp.dot(own_tile[:, :HD], q_cols, preferred_element_type=jnp.float32)
    own_at = lax.broadcasted_iota(jnp.int32, own.shape, 0)
    token_at = lax.broadcasted_iota(jnp.int32, own.shape, 1) % rlen
    return jnp.where(own_at <= token_at, own, -1e30)


def folded(values, op):
    return op(values.reshape(values.shape[0] // 8, 8, values.shape[1]), axis=0)


def turn(q_tile, per_kv, out_ref):
    out_ref[...] = stacked_heads(q_tile, per_kv).T


def finish(acc_ref, total_ref, length, per_kv, out_ref):
    out = (acc_ref[...] * (1.0 / total_ref[0:1, :])).T
    rlen = out_ref.shape[0]
    alive = lax.broadcasted_iota(jnp.int32, (rlen, HD), 0) < length
    for g in range(per_kv):
        part = jnp.where(alive, out[g * rlen:(g + 1) * rlen, :], 0.0)
        out_ref[:, g * HD:(g + 1) * HD] = part.astype(out_ref.dtype)


def scores_and_mix(q_cols, after_own, after_keys, after_s, after_u, after_peak, now):
    plen = after_keys.shape[0]
    scale = HD ** -0.5 * LOG2E
    own = own_scores(after_own, q_cols, after_own.shape[0])
    after_u[...] = own
    after_top = folded(own, jnp.max)
    if now is not None:
        s_ref, u_ref, peak_ref, own_tile, vt_ref, p_ref, acc_ref, total_ref = now
        peak = peak_ref[...]
        part = jnp.exp2((u_ref[...] - peak[0:1, :]) * scale)
        total = folded(part, jnp.sum)
        acc = lax.dot_general(own_tile[:, HD:], part.astype(jnp.bfloat16), TN, preferred_element_type=jnp.float32)
        spread = jnp.concatenate([peak] * (CHUNK // 8), axis=0)
    for at in range(0, plen, BLOCK):
        rows = pl.ds(at, BLOCK)
        if at % SCORE_BLOCK == 0:
            score_rows = pl.ds(at, SCORE_BLOCK)
            fresh = jnp.dot(after_keys[score_rows, :], q_cols, preferred_element_type=jnp.float32)
            after_s[score_rows, :] = fresh
            after_top = jnp.maximum(after_top, folded(fresh, jnp.max))
        if now is not None:
            for chunk in range(at, at + BLOCK, CHUNK):
                part = jnp.exp2((s_ref[chunk:chunk + CHUNK, :] - spread) * scale)
                total = total + folded(part, jnp.sum)
                p_ref[chunk:chunk + CHUNK, :] = part.astype(jnp.bfloat16)
            acc = acc + jnp.dot(vt_ref[:, rows], p_ref[rows, :], preferred_element_type=jnp.float32)
    after_peak[...] = jnp.broadcast_to(jnp.max(after_top, axis=0, keepdims=True), after_peak.shape)
    if now is not None:
        acc_ref[...] = acc
        total_ref[...] = jnp.broadcast_to(jnp.sum(total, axis=0, keepdims=True), total_ref.shape)


def listed(items, cap, count, facts, local, target, source, head):
    def look(at, n):
        hit = facts[GROUPS + at] == target

        @pl.when(hit)
        def _():
            items[n] = at
            items[cap + n] = source
            items[2 * cap + n] = facts[GROUPS + local + at]
            items[3 * cap + n] = head

        return n + hit.astype(jnp.int32)

    return lax.fori_loop(0, local, look, count)


def attend_kernel(passes, n_cand, per_kv, whole_head, two, fresh, waits, *refs):
    refs = list(refs)
    facts, refs = refs[0], refs[1:]
    if two:
        x_ref, refs = refs[0], refs[1:]
    q_ref, own_ref = refs[:2]
    cands, refs = refs[2:2 + n_cand], refs[2 + n_cand + waits:]
    n_out = 2 if two else 1
    if not fresh:
        refs = refs[1:]
    outs, token, refs = refs[:n_out], refs[n_out], refs[n_out + 1:]
    items, at_slot, q_buf, own_buf, key_buf, value_buf, vt_buf, s0, s1, u0, u1, peak0, peak1, turned0, turned1, acc0, acc1, total0, total1, p_buf, o0, o1, info, q_sem, own_sem, kv_sem, o_sem = refs
    s_buf, u_buf, peak_buf, o_buf = (s0, s1), (u0, u1), (peak0, peak1), (o0, o1)
    turned, acc_buf, total_buf = (turned0, turned1), (acc0, acc1), (total0, total1)
    local = (facts.shape[0] - GROUPS) // 2
    cap = items.shape[0] // 4
    width = per_kv * HD
    stacked = passes is None

    count = jnp.int32(0)
    if stacked:
        def one_prompt(prompt, n):
            return listed(items, cap, n, facts, local, prompt, prompt, whole_head)

        count = lax.fori_loop(0, cands[0].shape[0], one_prompt, count)
    else:
        for far, target, source, head in passes:
            if not far:
                count = listed(items, cap, count, facts, local, facts[target], facts[source], head)
                continue
            notes = pltpu.make_async_copy(x_ref.at[0, :, pl.ds(2 * (width + 2 * HD), HD)], info, kv_sem)
            notes.start()
            notes.wait()
            far_head = head
            handed = jnp.max(info[0:16, :].astype(jnp.float32)).astype(jnp.int32)
            handed = jnp.where(facts[target] >= 0, jnp.minimum(handed, SLOTS), 0)

            def take(slot, n):
                items[n] = local + slot
                items[cap + n] = facts[source]
                items[2 * cap + n] = q_buf.shape[1]
                items[3 * cap + n] = far_head
                return n + 1

            count = lax.fori_loop(0, handed, take, count)

    token[0] = count

    def each_array(i, act_local, act_far):
        at = items[i]
        if not two:
            act_local(at)
            return

        @pl.when(at < local)
        def _():
            act_local(at)

        @pl.when(at >= local)
        def _():
            act_far(at - local)

    first = pl.ds(0, width)

    def lanes(i, step, skip, size):
        return pl.ds(pl.multiple_of(items[3 * cap + i] * step + skip, HD), size)

    def mine(i):
        return lanes(i, width, 0, width)

    def fetch(i):
        slot, fourth = lax.rem(i, 2), lax.rem(i, 4)

        def here(at):
            pltpu.make_async_copy(q_ref.at[at, :, mine(i)], q_buf.at[slot], q_sem.at[slot]).start()
            pltpu.make_async_copy(own_ref.at[items[3 * cap + i], at], own_buf.at[fourth], own_sem.at[fourth]).start()

        def far(at):
            pltpu.make_async_copy(x_ref.at[at, :, lanes(i, width + 2 * HD, 0, width)], q_buf.at[slot], q_sem.at[slot]).start()
            pltpu.make_async_copy(x_ref.at[at, :, lanes(i, width + 2 * HD, width, 2 * HD)], own_buf.at[fourth], own_sem.at[fourth]).start()

        each_array(i, here, far)

    def fetched(i):
        slot, fourth = lax.rem(i, 2), lax.rem(i, 4)
        pltpu.make_async_copy(q_ref.at[0, :, first], q_buf.at[slot], q_sem.at[slot]).wait()
        pltpu.make_async_copy(own_ref.at[0, 0], own_buf.at[fourth], own_sem.at[fourth]).wait()

    def store(i, slot):
        def here(at):
            pltpu.make_async_copy(o_buf[slot], outs[0].at[at, :, mine(i)], o_sem.at[slot]).start()

        def far(at):
            pltpu.make_async_copy(o_buf[slot], outs[1].at[at], o_sem.at[slot]).start()

        each_array(i, here, far)

    def stored(slot):
        pltpu.make_async_copy(o_buf[slot], outs[0].at[0, :, first], o_sem.at[slot]).wait()

    keys, values = pl.ds(0, HD), pl.ds(HD, HD)

    def ask(i, into):
        source = items[cap + i]

        def bring(pairs):
            pltpu.make_async_copy(pairs.at[:, keys], key_buf.at[into], kv_sem).start()
            pltpu.make_async_copy(pairs.at[:, values], value_buf, kv_sem).start()

        if stacked:
            bring(cands[0].at[source])
        else:
            for which in range(n_cand):
                @pl.when(source == which)
                def _():
                    bring(cands[which].at[items[3 * cap + i]] if len(cands[which].shape) == 3 else cands[which])

    def receive(into):
        for _ in range(2):
            pltpu.make_async_copy(value_buf, value_buf, kv_sem).wait()
        vt_buf[into] = value_buf[...].T

    @pl.when(count > 0)
    def _():
        ask(0, 0)
        fetch(jnp.int32(0))

        @pl.when(count > 1)
        def _():
            fetch(jnp.int32(1))

        at_slot[0] = 0
        fetched(jnp.int32(0))
        turn(q_buf[0], per_kv, turned[0])

        @pl.when(count > 2)
        def _():
            fetch(jnp.int32(2))

        @pl.when(count > 1)
        def _():
            fetched(jnp.int32(1))

        turn(q_buf[1], per_kv, turned[1])
        receive(0)
        scores_and_mix(turned[0][...], own_buf[0], key_buf.at[0], s_buf[0], u_buf[0], peak_buf[0], None)

        def one(i, slot):
            other = 1 - slot
            held = at_slot[0]
            more = i + 1 < count
            after_i = jnp.minimum(i + 1, count - 1)
            moved = more & ((items[cap + after_i] != items[cap + i]) | (items[3 * cap + after_i] != items[3 * cap + i]))
            holds = jnp.where(moved, 1 - held, held)
            at_slot[0] = holds

            @pl.when(i + 2 < count)
            def _():
                fetched(i + 2)

            @pl.when(i + 3 < count)
            def _():
                fetch(i + 3)

            @pl.when(moved)
            def _():
                ask(i + 1, holds)
                receive(holds)

            @pl.when(i >= 3)
            def _():
                stored(other)

            now = (
                s_buf[slot], u_buf[slot], peak_buf[slot], own_buf[lax.rem(i, 4)], vt_buf.at[held], p_buf,
                acc_buf[slot], total_buf[slot])
            scores_and_mix(
                turned[other][...], own_buf[lax.rem(i + 1, 4)], key_buf.at[holds],
                s_buf[other], u_buf[other], peak_buf[other], now)
            turn(q_buf[slot], per_kv, turned[slot])
            finish(acc_buf[other], total_buf[other], items[2 * cap + jnp.maximum(i - 1, 0)], per_kv, o_buf[other])

            @pl.when(i >= 1)
            def _():
                store(i - 1, other)

        def pair(j, _):
            one(2 * j, 0)

            @pl.when(2 * j + 1 < count)
            def _():
                one(2 * j + 1, 1)

            return 0

        lax.fori_loop(0, lax.div(count + 1, 2), pair, 0)
        final = count - 1
        for slot in range(2):
            @pl.when(lax.rem(final, 2) == slot)
            def _():
                @pl.when(final >= 2)
                def _():
                    stored(slot)

                finish(acc_buf[slot], total_buf[slot], items[2 * cap + final], per_kv, o_buf[slot])
                store(final, slot)

        stored(0)

        @pl.when(count > 1)
        def _():
            stored(1)


def attend(facts, queries, own, cands, outs, head, per_kv, passes, items, far=None, fresh=False, wait_for=None):
    rlen = queries.shape[1]
    plen = cands[0].shape[-2]
    width = per_kv * HD
    small = [facts]
    large = ([far] if far is not None else []) + [queries, own] + cands
    operands = small + large + ([] if wait_for is None else [wait_for])
    aliases = {}
    if not fresh:
        aliases = {len(operands): 0}
        operands = operands + [outs[0]]
    cap = 2 * queries.shape[0] + (SLOTS if far is not None else 0)
    return pl.pallas_call(
        functools.partial(attend_kernel, passes, len(cands), per_kv, head, far is not None, fresh, wait_for is not None),
        out_shape=[jax.ShapeDtypeStruct(o.shape, o.dtype) for o in outs] + [jax.ShapeDtypeStruct((1,), jnp.int32)],
        in_specs=[SMEM] * len(small) + [HBM] * (len(operands) - len(small)),
        out_specs=[HBM] * len(outs) + [SMEM],
        input_output_aliases=aliases,
        scratch_shapes=[
            pltpu.SMEM((4 * cap,), jnp.int32),
            pltpu.SMEM((1,), jnp.int32),
            pltpu.VMEM((2, rlen, width), jnp.bfloat16),
            pltpu.VMEM((4, rlen, 2 * HD), jnp.bfloat16),
            pltpu.VMEM((2, plen, HD), jnp.bfloat16),
            pltpu.VMEM((plen, HD), jnp.bfloat16),
            pltpu.VMEM((2, HD, plen), jnp.bfloat16),
            pltpu.VMEM((plen, per_kv * rlen), jnp.float32),
            pltpu.VMEM((plen, per_kv * rlen), jnp.float32),
            pltpu.VMEM((rlen, per_kv * rlen), jnp.float32),
            pltpu.VMEM((rlen, per_kv * rlen), jnp.float32),
            pltpu.VMEM((8, per_kv * rlen), jnp.float32),
            pltpu.VMEM((8, per_kv * rlen), jnp.float32),
            pltpu.VMEM((HD, per_kv * rlen), jnp.bfloat16),
            pltpu.VMEM((HD, per_kv * rlen), jnp.bfloat16),
            pltpu.VMEM((HD, per_kv * rlen), jnp.float32),
            pltpu.VMEM((HD, per_kv * rlen), jnp.float32),
            pltpu.VMEM((8, per_kv * rlen), jnp.float32),
            pltpu.VMEM((8, per_kv * rlen), jnp.float32),
            pltpu.VMEM((plen, per_kv * rlen), jnp.bfloat16),
            pltpu.VMEM((rlen, width), jnp.bfloat16),
            pltpu.VMEM((rlen, width), jnp.bfloat16),
            pltpu.VMEM((rlen, HD), jnp.bfloat16),
            pltpu.SemaphoreType.DMA((2,)),
            pltpu.SemaphoreType.DMA((4,)),
            pltpu.SemaphoreType.DMA,
            pltpu.SemaphoreType.DMA((2,)),
        ],
        compiler_params=pltpu.CompilerParams(vmem_limit_bytes=VMEM_BYTES),
        cost_estimate=pl.CostEstimate(flops=items << 20, bytes_accessed=1 << 16, transcendentals=0),
    )(*operands)


def pack_kernel(target, width, facts, q_ref, own_ref, out, sem):
    step = width + 2 * HD
    local = q_ref.shape[0]

    def each(act):
        def look(at, slot):
            hit = facts[GROUPS + at] == facts[target]

            @pl.when(hit)
            def _():
                for head in range(2):
                    part = pl.ds(head * width, width)
                    act(pltpu.make_async_copy(q_ref.at[at, :, part], out.at[slot, :, pl.ds(head * step, width)], sem))
                    act(pltpu.make_async_copy(
                        own_ref.at[head, at], out.at[slot, :, pl.ds(head * step + width, 2 * HD)], sem))

            return slot + hit.astype(jnp.int32)

        return lax.fori_loop(0, local, look, jnp.int32(0))

    count = each(lambda copy: copy.start())
    out[0, :, 2 * step:] = jnp.full((out.shape[1], HD), count, jnp.int32).astype(jnp.float32).astype(out.dtype)
    each(lambda copy: copy.wait())


def pack(facts, target, queries, own, width):
    return pl.pallas_call(
        functools.partial(pack_kernel, target, width),
        out_shape=jax.ShapeDtypeStruct((SLOTS, queries.shape[1], 2 * width + 5 * HD), queries.dtype),
        in_specs=[SMEM, HBM, HBM],
        out_specs=VMEM,
        scratch_shapes=[pltpu.SemaphoreType.DMA],
        compiler_params=pltpu.CompilerParams(vmem_limit_bytes=1 << 23),
    )(facts, queries, own)


def gate_kernel(*refs):
    pass


def gate(value, *others):
    return pl.pallas_call(
        gate_kernel,
        out_shape=jax.ShapeDtypeStruct(value.shape, value.dtype),
        in_specs=[HBM] + [SMEM if other.ndim == 1 else HBM for other in others],
        out_specs=HBM,
        input_output_aliases={0: 0},
    )(value, *others)


def cut_kernel(pair, out0, out1, sem):
    copies = [pltpu.make_async_copy(pair.at[head], out, sem.at[head]) for head, out in enumerate((out0, out1))]
    for copy in copies:
        copy.start()
    for copy in copies:
        copy.wait()


def cut(pair):
    shape = jax.ShapeDtypeStruct(pair.shape[1:], pair.dtype)
    return pl.pallas_call(
        cut_kernel,
        out_shape=[shape, shape],
        in_specs=[HBM],
        out_specs=[VMEM, VMEM],
        scratch_shapes=[pltpu.SemaphoreType.DMA((2,))],
        compiler_params=pltpu.CompilerParams(vmem_limit_bytes=1 << 23),
    )(pair)


def merge_kernel(target, head, facts, groups, lengths, got, old, out, ready, sem):
    rlen, width = got.shape[1:]
    token_at = lax.broadcasted_iota(jnp.int32, (rlen, HD), 0)

    def each(act, fill):
        def look(at, slot):
            hit = groups[at] == facts[target]

            @pl.when(hit)
            def _():
                if fill:
                    alive = token_at < lengths[at]
                    for lane in range(0, width, HD):
                        part = got[slot, :, lane:lane + HD]
                        ready[slot, :, lane:lane + HD] = jnp.where(alive, part, jnp.zeros_like(part))
                act(pltpu.make_async_copy(ready.at[slot], out.at[at, :, pl.ds(head * width, width)], sem))

            return slot + hit.astype(jnp.int32)

        lax.fori_loop(0, groups.shape[0], look, jnp.int32(0))

    each(lambda copy: copy.start(), True)
    each(lambda copy: copy.wait(), False)


def merge(facts, target, groups, lengths, got, out, head):
    return pl.pallas_call(
        functools.partial(merge_kernel, target, head),
        out_shape=jax.ShapeDtypeStruct(out.shape, out.dtype),
        in_specs=[SMEM, SMEM, SMEM, VMEM, HBM],
        out_specs=HBM,
        input_output_aliases={4: 0},
        scratch_shapes=[pltpu.VMEM(got.shape, got.dtype), pltpu.SemaphoreType.DMA],
        compiler_params=pltpu.CompilerParams(vmem_limit_bytes=1 << 23),
    )(facts, groups, lengths, got, out)


def after(value, *others):
    return lax.optimization_barrier((value,) + others)[0]


def gathered(queries, resp_kv, prompt_kv, lengths, group_of, first_head, kv_needed, per_kv):
    out = jax.ShapeDtypeStruct(queries.shape, jnp.bfloat16)
    facts = jnp.concatenate([jnp.zeros((GROUPS,), jnp.int32), group_of, lengths])
    for head in range(kv_needed):
        mine = lax.dynamic_index_in_dim(prompt_kv, first_head + head, 2, keepdims=False)
        own = lax.dynamic_index_in_dim(resp_kv, first_head + head, 2, keepdims=False)[None]
        whole = lax.all_gather(mine, "seq", axis=0, tiled=True)
        out, _ = attend(facts, queries, own, [whole], [out], head, per_kv, None, 16, fresh=head == 0)
    return out


def relayed(queries, resp_kv, prompt_kv, lengths, group_of, first_head, per_kv):
    me = lax.axis_index("seq")
    width = per_kv * HD
    middle, inward, outward = [(1, 2), (2, 1)], [(0, 1), (3, 2)], [(1, 0), (2, 3)]

    def send(pairs, value):
        return lax.ppermute(value, "seq", pairs)

    def two_heads(start):
        return lambda pairs: jnp.transpose(pairs[:, start:start + 2], (1, 0, 2))

    def two_own(start):
        return lambda pairs: jnp.transpose(pairs[:, :, start:start + 2], (2, 0, 1, 3))

    splits = prompt_kv.shape[2] // 2
    mine = lax.switch(first_head // 2, [two_heads(2 * at) for at in range(splits)], prompt_kv[0])
    inner_prompt = send(outward, mine)
    parts = cut(mine)
    across, near = [], []
    for part in parts:
        across.append(send(middle, part))
        near.append(send(inward, part))

    low = me < 2
    is_inner = (me == 1) | (me == 2)
    outer, inner = jnp.where(low, 0, 3), jnp.where(low, 1, 2)
    far_inner, far_outer = jnp.where(low, 2, 1), jnp.where(low, 3, 0)
    facts = jnp.stack([
        me,
        jnp.zeros_like(me),
        jnp.where(is_inner, -1, inner),
        jnp.full_like(me, 3),
        jnp.where(is_inner, far_inner, -1),
        jnp.ones_like(me),
        jnp.where(is_inner, far_outer, -1),
        jnp.where(is_inner, far_outer, far_inner),
        jnp.where(is_inner, 0, 1),
        jnp.where(is_inner, -1, far_outer),
        jnp.where(is_inner, outer, -1),
        jnp.full_like(me, 2),
    ]).astype(jnp.int32)
    facts = jnp.concatenate([facts, group_of, lengths])

    own = lax.switch(first_head // 2, [two_own(2 * at) for at in range(splits)], resp_kv)
    packed = pack(facts, 9, queries, own, width)
    out = jax.ShapeDtypeStruct(queries.shape, jnp.bfloat16)
    back_shape = jax.ShapeDtypeStruct((SLOTS, queries.shape[1], width), jnp.bfloat16)

    def run(cands, outs, passes, items, far=None, fresh=False, wait_for=None):
        return attend(facts, queries, own, cands, outs, 0, per_kv, passes, items, far, fresh, wait_for)

    out, token = run([mine], [out], [(False, 0, 1, 0), (False, 0, 1, 1)], 8, fresh=True, wait_for=packed)
    near[0] = gate(near[0], token)
    last = [send(middle, near[0])]
    handed = send(inward, gate(packed, near[0]))
    out, token = run([near[0]], [out], [(False, 10, 1, 0)], 4)
    across[0] = gate(across[0], token, inner_prompt)
    far_inner_prompt = [send(outward, across[0])]
    near[1] = gate(near[1], token)
    last.append(send(middle, near[1]))
    across[1] = gate(across[1], token)
    far_inner_prompt.append(send(outward, across[1]))
    out, _ = run(
        [near[1], across[0], across[1], inner_prompt], [out],
        [(False, 2, 3, 0), (False, 2, 3, 1), (False, 10, 1, 1), (False, 4, 5, 0), (False, 4, 11, 1)], 16, wait_for=near[1])
    back = [None, None]
    out, back[0], _ = run(
        [last[0], far_inner_prompt[0]], [out, back_shape], [(True, 6, 1, 0), (False, 7, 8, 0)], 8, handed)
    back[0] = send(outward, back[0])
    out, back[1], _ = run([last[1]], [out, back_shape], [(True, 6, 1, 1)], 4, handed)
    back[1] = send(outward, back[1])
    out, _ = run([last[1], far_inner_prompt[1]], [out], [(False, 7, 8, 1)], 4)
    for head in range(2):
        out = merge(facts, 9, group_of, lengths, back[head], out, head)
    return out


def shards(queries, resp_kv, prompt_kv, lengths, group_of):
    local_heads = queries.shape[2] // HD
    group = QHEADS // KVH
    kv_needed = max(local_heads // group, 1)
    per_kv = local_heads // kv_needed
    first_head = lax.axis_index("pp") * local_heads // group
    args = (queries, resp_kv, prompt_kv, lengths, group_of, first_head)
    if lax.axis_size("seq") == 4 and kv_needed == 2 and prompt_kv.shape[0] == 1:
        return relayed(*args, per_kv)
    return gathered(*args, kv_needed, per_kv)


def solution(mesh):
    placed = (
        P(("rep", "seq"), None, ("tp", "pp")),
        P(("rep", "seq"), None, "tp", None),
        P(("rep", "seq"), None, "tp", None),
        P(("rep", "seq")),
        P(("rep", "seq")),
    )
    return jax.shard_map(
        shards,
        mesh=mesh,
        in_specs=placed,
        out_specs=P(("rep", "seq"), None, ("tp", "pp")),
        check_vma=False,
    )
```

profile of v0, /device:TPU:4, one launch (start us, length us, event | category | flops | bytes accessed | tf_op | source)
XLA Modules:
  0.0 133.7 jit_solution(8716287125590448037)
XLA Ops:
  0.0 5.2 %conditional.3 = (bf16[2,2048,256]{2,1,0:T(8,128)(2,1)}) conditional(s32[]{:T(128)} %clamp.4, bf16[2048,4,256]{2,1,0:T(4,128)(2,1)} %bitcast.17, bf16[2048,4,256]{2,1,0:T(4,128)(2,1)} %bitcast.18), branch_computations={%region_2.3_spmd, %region_3.4_spmd} | conditional | bytes 8388616 | solution.py:508
  0.0 3.6 %slice_bitcast_fusion.2 = bf16[2,2048,256]{2,0,1:T(2,128)(2,1)S(1)} fusion(bf16[2048,4,256]{2,1,0:T(4,128)(2,1)} %param.2), kind=kLoop, calls=%fused_computation.2 | loop fusion | bytes 4194304 | tf_op jit(solution)/shard_map/cond/branch_0_fun/transpose | solution.py:502
  3.7 1.6 %copy.30 = bf16[2,2048,256]{2,1,0:T(8,128)(2,1)} copy(bf16[2,2048,256]{2,0,1:T(2,128)(2,1)S(1)} %slice_bitcast_fusion.2) | data formatting | bytes 4194304 | tf_op jit(solution)/shard_map/cond | solution.py:508
  5.2 1.4 %collective-permute-start.6 = (bf16[2,2048,256]{2,1,0:T(8,128)(2,1)}, bf16[2,2048,256]{2,1,0:T(8,128)(2,1)}, u32[]{:S(2)}, u32[]{:S(2)}) collective-permute-start(bf16[2,2048,256]{2,1,0:T(8,128)(2,1)} %get-tuple-element.40.pair.refs_3_), channel_id=1, source_target_pairs={{4,0},{8,12},{5,1},{9,13},{6,2},{10,14},{7,3},{11,15},{20,16},{24,... | collective-permute-start | bytes 6291464 | tf_op jit(solution)/shard_map/ppermute | solution.py:499
  6.6 2.9 %shard_map.62 = (bf16[2048,256]{1,0:T(8,128)(2,1)}, bf16[2048,256]{1,0:T(8,128)(2,1)}) custom-call(bf16[2,2048,256]{2,1,0:T(8,128)(2,1)} %get-tuple-element.40.pair.refs_3_), custom_call_target="tpu_custom_call" | custom-call | tf_op jit(solution)/shard_map/pallas_call | solution.py:431
  9.6 6.8 %collective-permute-start = (bf16[2048,256]{1,0:T(8,128)(2,1)}, bf16[2048,256]{1,0:T(8,128)(2,1)}, u32[]{:S(2)}, u32[]{:S(2)}) collective-permute-start(bf16[2048,256]{1,0:T(8,128)(2,1)} %get-tuple-element.27), channel_id=1, source_target_pairs={{0,4},{12,8},{1,5},{13,9},{2,6},{14,10},{3,7},{15,11},{16,20},{28,... | collective-permute-start | bytes 3145736 | tf_op jit(solution)/shard_map/ppermute | solution.py:499
  16.4 1.6 %collective-permute-start.5 = (bf16[2048,256]{1,0:T(8,128)(2,1)}, bf16[2048,256]{1,0:T(8,128)(2,1)}, u32[]{:S(2)}, u32[]{:S(2)}) collective-permute-start(bf16[2048,256]{1,0:T(8,128)(2,1)} %get-tuple-element.27), channel_id=1, source_target_pairs={{4,8},{8,4},{5,9},{9,5},{6,10},{10,6},{7,11},{11,7},{20,24},{24,20... | collective-permute-start | bytes 3145736 | tf_op jit(solution)/shard_map/ppermute | solution.py:499
  18.0 4.4 %collective-permute-start.2 = (bf16[2048,256]{1,0:T(8,128)(2,1)}, bf16[2048,256]{1,0:T(8,128)(2,1)}, u32[]{:S(2)}, u32[]{:S(2)}) collective-permute-start(bf16[2048,256]{1,0:T(8,128)(2,1)} %get-tuple-element.29), channel_id=1, source_target_pairs={{0,4},{12,8},{1,5},{13,9},{2,6},{14,10},{3,7},{15,11},{16,20},{28,... | collective-permute-start | bytes 3145736 | tf_op jit(solution)/shard_map/ppermute | solution.py:499
  22.4 1.6 %collective-permute-start.8 = (bf16[2048,256]{1,0:T(8,128)(2,1)}, bf16[2048,256]{1,0:T(8,128)(2,1)}, u32[]{:S(2)}, u32[]{:S(2)}) collective-permute-start(bf16[2048,256]{1,0:T(8,128)(2,1)} %get-tuple-element.29), channel_id=1, source_target_pairs={{4,8},{8,4},{5,9},{9,5},{6,10},{10,6},{7,11},{11,7},{20,24},{24,20... | collective-permute-start | bytes 3145736 | tf_op jit(solution)/shard_map/ppermute | solution.py:499
  24.0 0.5 conditional.2
  24.1 0.4 slice_bitcast_fusion
  24.5 0.1 copy.28
  24.6 0.1 copy-done.2
  24.7 0.0 copy-done.3
  24.7 0.1 concatenate.3.facts.refs_0_
  24.8 1.0 copy-done
  25.8 1.3 shard_map.61.refs_4_.refs_0_
  27.2 1.5 %shard_map.63 = (bf16[16,32,2048]{2,1,0:T(8,128)(2,1)}, s32[1]{0:T(128)}) custom-call(s32[44]{0:T(128)S(1)} %concatenate.3.facts.refs_0_, bf16[16,32,2048]{2,1,0:T(8,128)(2,1)S(1)} %copy-done, bf16[2,16,32,256]{3,2,1,0:T(8,128)(2,1)S(1)} %get-tuple-element.39.own_ref.refs_2_.refs_3_, bf16[2,2048,256]{2,1,0:T(8,128)(2,1)} %get-tuple-element.40.pair.refs_3_, ...), custom_call_target="tpu_custom_call" | custom-call | flops 8388608 | bytes 65536 | tf_op jit(solution)/shard_map/pallas_call | solution.py:331
  28.7 10.5 %collective-permute-done.refs_0_ = bf16[2048,256]{1,0:T(8,128)(2,1)} collective-permute-done((bf16[2048,256]{1,0:T(8,128)(2,1)}, bf16[2048,256]{1,0:T(8,128)(2,1)}, u32[]{:S(2)}, u32[]{:S(2)}) %collective-permute-start) | collective-permute-done | bytes 1048608 | tf_op jit(solution)/shard_map/ppermute | solution.py:499
  39.3 0.6 shard_map.64.refs_1_.refs_3_
  39.9 4.5 %collective-permute-start.1 = (bf16[8,32,2688]{2,1,0:T(8,128)(2,1)}, bf16[8,32,2688]{2,1,0:T(8,128)(2,1)S(1)}, u32[]{:S(2)}, u32[]{:S(2)}) collective-permute-start(bf16[8,32,2688]{2,1,0:T(8,128)(2,1)} %shard_map.65), channel_id=1, source_target_pairs={{0,4},{12,8},{1,5},{13,9},{2,6},{14,10},{3,7},{15,11},{16,20},{28,... | collective-permute-start | bytes 4128776 | tf_op jit(solution)/shard_map/ppermute | solution.py:499
  44.4 1.3 shard_map.66
  45.7 0.0 collective-permute-done.5.refs_0_
  45.8 1.7 %collective-permute-start.4 = (bf16[2048,256]{1,0:T(8,128)(2,1)}, bf16[2048,256]{1,0:T(8,128)(2,1)}, u32[]{:S(2)}, u32[]{:S(2)}) collective-permute-start(bf16[2048,256]{1,0:T(8,128)(2,1)} %shard_map.64.refs_1_.refs_3_), channel_id=1, source_target_pairs={{4,8},{8,4},{5,9},{9,5},{6,10},{10,6},{7,11},{11,7},{20,24},{24,20... | collective-permute-start | bytes 3145736 | tf_op jit(solution)/shard_map/ppermute | solution.py:499
  47.4 8.1 %collective-permute-done.6.refs_2_.refs_6_ = bf16[2,2048,256]{2,1,0:T(8,128)(2,1)} collective-permute-done((bf16[2,2048,256]{2,1,0:T(8,128)(2,1)}, bf16[2,2048,256]{2,1,0:T(8,128)(2,1)}, u32[]{:S(2)}, u32[]{:S(2)}) %collective-permute-start.6) | collective-permute-done | bytes 2097184 | tf_op jit(solution)/shard_map/ppermute | solution.py:499
  55.5 0.6 shard_map.68.refs_4_
  56.2 1.3 collective-permute-start.7
  57.5 4.3 %collective-permute-done.2.refs_0_ = bf16[2048,256]{1,0:T(8,128)(2,1)} collective-permute-done((bf16[2048,256]{1,0:T(8,128)(2,1)}, bf16[2048,256]{1,0:T(8,128)(2,1)}, u32[]{:S(2)}, u32[]{:S(2)}) %collective-permute-start.2) | collective-permute-done | bytes 1048608 | tf_op jit(solution)/shard_map/ppermute | solution.py:499
  61.7 0.6 shard_map.67.refs_3_.refs_7_
  62.4 1.6 %collective-permute-start.3 = (bf16[2048,256]{1,0:T(8,128)(2,1)}, bf16[2048,256]{1,0:T(8,128)(2,1)}, u32[]{:S(2)}, u32[]{:S(2)}) collective-permute-start(bf16[2048,256]{1,0:T(8,128)(2,1)} %shard_map.67.refs_3_.refs_7_), channel_id=1, source_target_pairs={{4,8},{8,4},{5,9},{9,5},{6,10},{10,6},{7,11},{11,7},{20,24},{24,20... | collective-permute-start | bytes 3145736 | tf_op jit(solution)/shard_map/ppermute | solution.py:499
  64.0 0.0 collective-permute-done.8.refs_0_
  64.0 0.6 shard_map.69.refs_5_
  64.6 1.3 collective-permute-start.11
  65.9 7.2 %shard_map.70 = (bf16[16,32,2048]{2,1,0:T(8,128)(2,1)}, s32[1]{0:T(128)}) custom-call(s32[44]{0:T(128)S(1)} %concatenate.3.facts.refs_0_, bf16[16,32,2048]{2,1,0:T(8,128)(2,1)S(1)} %copy-done, bf16[2,16,32,256]{3,2,1,0:T(8,128)(2,1)} %copy-done.4, bf16[2048,256]{1,0:T(8,128)(2,1)} %shard_map.67.refs_3_.refs_7_, ...), custom_call_target="tpu_custom_call", output_to_operand_aliasing={{0}: (8, {})} | custom-call | flops 16777216 | bytes 65536 | tf_op jit(solution)/shard_map/pallas_call | solution.py:331
  73.1 0.0 collective-permute-done.4.refs_4_
  73.1 17.3 %collective-permute-done.1.refs_1_ = bf16[8,32,2688]{2,1,0:T(8,128)(2,1)S(1)} collective-permute-done((bf16[8,32,2688]{2,1,0:T(8,128)(2,1)}, bf16[8,32,2688]{2,1,0:T(8,128)(2,1)S(1)}, u32[]{:S(2)}, u32[]{:S(2)}) %collective-permute-start.1) | collective-permute-done | bytes 1376288 | tf_op jit(solution)/shard_map/ppermute | solution.py:499
  90.4 0.0 collective-permute-done.7.refs_5_
  90.4 9.3 %shard_map.71 = (bf16[16,32,2048]{2,1,0:T(8,128)(2,1)}, bf16[8,32,1024]{2,1,0:T(8,128)(2,1)S(1)}, s32[1]{0:T(128)}) custom-call(s32[44]{0:T(128)S(1)} %concatenate.3.facts.refs_0_, bf16[8,32,2688]{2,1,0:T(8,128)(2,1)S(1)} %collective-permute-done.1.refs_1_, bf16[16,32,2048]{2,1,0:T(8,128)(2,1)S(1)} %copy-done, ...), custom_call_target="tpu_custom_call", output_to_operand_aliasing={{0}: (6, {})} | custom-call | flops 8388608 | bytes 65536 | tf_op jit(solution)/shard_map/pallas_call | solution.py:331
  99.8 1.3 collective-permute-start.10
  101.1 0.0 collective-permute-done.3.refs_4_.refs_3_
  101.1 1.3 shard_map.72
  102.4 1.3 collective-permute-start.9
  103.7 1.7 %collective-permute-done.11.refs_4_ = bf16[2048,256]{1,0:T(8,128)(2,1)S(1)} collective-permute-done((bf16[2048,256]{1,0:T(8,128)(2,1)}, bf16[2048,256]{1,0:T(8,128)(2,1)S(1)}, u32[]{:S(2)}, u32[]{:S(2)}) %collective-permute-start.11) | collective-permute-done | bytes 1048608 | tf_op jit(solution)/shard_map/ppermute | solution.py:499
  105.4 8.4 %shard_map.73 = (bf16[16,32,2048]{2,1,0:T(8,128)(2,1)}, s32[1]{0:T(128)}) custom-call(s32[44]{0:T(128)S(1)} %concatenate.3.facts.refs_0_, bf16[16,32,2048]{2,1,0:T(8,128)(2,1)S(1)} %copy-done, bf16[2,16,32,256]{3,2,1,0:T(8,128)(2,1)S(1)} %copy-done.5, bf16[2048,256]{1,0:T(8,128)(2,1)} %collective-permute-done.3.refs_4_.refs_3_, ...), custom_call_target="tpu_custom_call", output_to_operand_aliasing={{0}: (5, {})} | custom-call | flops 4194304 | bytes 65536 | tf_op jit(solution)/shard_map/pallas_call | solution.py:331
  113.8 6.7 %collective-permute-done.10.got = bf16[8,32,1024]{2,1,0:T(8,128)(2,1)S(1)} collective-permute-done((bf16[8,32,1024]{2,1,0:T(8,128)(2,1)S(1)}, bf16[8,32,1024]{2,1,0:T(8,128)(2,1)S(1)}, u32[]{:S(2)}, u32[]{:S(2)}) %collective-permute-start.10) | collective-permute-done | bytes 524320 | tf_op jit(solution)/shard_map/ppermute | solution.py:499
  120.5 1.5 %shard_map.74.old = bf16[16,32,2048]{2,1,0:T(8,128)(2,1)} custom-call(s32[44]{0:T(128)S(1)} %concatenate.3.facts.refs_0_, s32[16]{0:T(128)S(1)} %copy-done.2, s32[16]{0:T(128)S(1)} %copy-done.3, bf16[8,32,1024]{2,1,0:T(8,128)(2,1)S(1)} %collective-permute-done.10.got, bf16[16,32,2048]{2,1,0:T(8,128)(2,1)} %get-tuple-element.38.old), custom_call_target="tpu_custom_call", output_to_operand_aliasing={{}: (4, {})} | custom-call | tf_op jit(solution)/shard_map/pallas_call | solution.py:467
  122.1 10.0 %collective-permute-done.9.got = bf16[8,32,1024]{2,1,0:T(8,128)(2,1)S(1)} collective-permute-done((bf16[8,32,1024]{2,1,0:T(8,128)(2,1)S(1)}, bf16[8,32,1024]{2,1,0:T(8,128)(2,1)S(1)}, u32[]{:S(2)}, u32[]{:S(2)}) %collective-permute-start.9) | collective-permute-done | bytes 524320 | tf_op jit(solution)/shard_map/ppermute | solution.py:499
  132.1 1.5 %shard_map.75 = bf16[16,32,2048]{2,1,0:T(8,128)(2,1)} custom-call(s32[44]{0:T(128)S(1)} %concatenate.3.facts.refs_0_, s32[16]{0:T(128)S(1)} %copy-done.2, s32[16]{0:T(128)S(1)} %copy-done.3, bf16[8,32,1024]{2,1,0:T(8,128)(2,1)S(1)} %collective-permute-done.9.got, bf16[16,32,2048]{2,1,0:T(8,128)(2,1)} %shard_map.74.old), custom_call_target="tpu_custom_call", output_to_operand_aliasing={{}: (4, {})} | custom-call | tf_op jit(solution)/shard_map/pallas_call | solution.py:467
  (12 shorter events, 0.0 us)
Async XLA Ops:
  5.2 18.8 %copy-start.6 = (bf16[16,32,4,256]{3,2,1,0:T(4,128)(2,1)S(1)}, bf16[16,32,4,256]{3,2,1,0:T(4,128)(2,1)}, u32[]{:S(2)}) copy-start(bf16[16,32,4,256]{3,2,1,0:T(4,128)(2,1)} %param.10) | copy-start | bytes 3145732
  5.2 50.3 %collective-permute-start.6 = (bf16[2,2048,256]{2,1,0:T(8,128)(2,1)}, bf16[2,2048,256]{2,1,0:T(8,128)(2,1)}, u32[]{:S(2)}, u32[]{:S(2)}) collective-permute-start(bf16[2,2048,256]{2,1,0:T(8,128)(2,1)} %get-tuple-element.40.pair.refs_3_), channel_id=1, source_target_pairs={{4,0},{8,12},{5,1},{9,13},{6,2},{10,14},{7,3},{11,15},{20,16},{24,... | collective-permute-start | bytes 6291464 | tf_op jit(solution)/shard_map/ppermute | solution.py:499
  9.6 29.7 %collective-permute-start = (bf16[2048,256]{1,0:T(8,128)(2,1)}, bf16[2048,256]{1,0:T(8,128)(2,1)}, u32[]{:S(2)}, u32[]{:S(2)}) collective-permute-start(bf16[2048,256]{1,0:T(8,128)(2,1)} %get-tuple-element.27), channel_id=1, source_target_pairs={{0,4},{12,8},{1,5},{13,9},{2,6},{14,10},{3,7},{15,11},{16,20},{28,... | collective-permute-start | bytes 3145736 | tf_op jit(solution)/shard_map/ppermute | solution.py:499
  16.4 29.3 %collective-permute-start.5 = (bf16[2048,256]{1,0:T(8,128)(2,1)}, bf16[2048,256]{1,0:T(8,128)(2,1)}, u32[]{:S(2)}, u32[]{:S(2)}) collective-permute-start(bf16[2048,256]{1,0:T(8,128)(2,1)} %get-tuple-element.27), channel_id=1, source_target_pairs={{4,8},{8,4},{5,9},{9,5},{6,10},{10,6},{7,11},{11,7},{20,24},{24,20... | collective-permute-start | bytes 3145736 | tf_op jit(solution)/shard_map/ppermute | solution.py:499
  18.0 43.7 %collective-permute-start.2 = (bf16[2048,256]{1,0:T(8,128)(2,1)}, bf16[2048,256]{1,0:T(8,128)(2,1)}, u32[]{:S(2)}, u32[]{:S(2)}) collective-permute-start(bf16[2048,256]{1,0:T(8,128)(2,1)} %get-tuple-element.29), channel_id=1, source_target_pairs={{0,4},{12,8},{1,5},{13,9},{2,6},{14,10},{3,7},{15,11},{16,20},{28,... | collective-permute-start | bytes 3145736 | tf_op jit(solution)/shard_map/ppermute | solution.py:499
  22.4 41.6 %collective-permute-start.8 = (bf16[2048,256]{1,0:T(8,128)(2,1)}, bf16[2048,256]{1,0:T(8,128)(2,1)}, u32[]{:S(2)}, u32[]{:S(2)}) collective-permute-start(bf16[2048,256]{1,0:T(8,128)(2,1)} %get-tuple-element.29), channel_id=1, source_target_pairs={{4,8},{8,4},{5,9},{9,5},{6,10},{10,6},{7,11},{11,7},{20,24},{24,20... | collective-permute-start | bytes 3145736 | tf_op jit(solution)/shard_map/ppermute | solution.py:499
  24.0 0.7 copy-start.2
  24.0 0.7 copy-start.3
  24.0 1.8 %copy-start = (bf16[16,32,2048]{2,1,0:T(8,128)(2,1)S(1)}, bf16[16,32,2048]{2,1,0:T(8,128)(2,1)}, u32[]{:S(2)}) copy-start(bf16[16,32,2048]{2,1,0:T(8,128)(2,1)} %refs_1_.7) | copy-start | bytes 6291460
  24.6 15.3 %copy-start.4 = (bf16[2,16,32,256]{3,2,1,0:T(8,128)(2,1)}, bf16[2,16,32,256]{3,2,1,0:T(8,128)(2,1)S(1)}, u32[]{:S(2)}) copy-start(bf16[2,16,32,256]{3,2,1,0:T(8,128)(2,1)S(1)} %get-tuple-element.39.own_ref.refs_2_.refs_3_) | copy-start | bytes 1572868
  27.2 1.5 %copy-start.1 = (bf16[8,32,2688]{2,1,0:T(8,128)(2,1)}, bf16[8,32,2688]{2,1,0:T(8,128)(2,1)S(1)}, u32[]{:S(2)}) copy-start(bf16[8,32,2688]{2,1,0:T(8,128)(2,1)S(1)} %shard_map.61.refs_4_.refs_0_) | copy-start | bytes 4128772
  39.9 50.5 %collective-permute-start.1 = (bf16[8,32,2688]{2,1,0:T(8,128)(2,1)}, bf16[8,32,2688]{2,1,0:T(8,128)(2,1)S(1)}, u32[]{:S(2)}, u32[]{:S(2)}) collective-permute-start(bf16[8,32,2688]{2,1,0:T(8,128)(2,1)} %shard_map.65), channel_id=1, source_target_pairs={{0,4},{12,8},{1,5},{13,9},{2,6},{14,10},{3,7},{15,11},{16,20},{28,... | collective-permute-start | bytes 4128776 | tf_op jit(solution)/shard_map/ppermute | solution.py:499
  45.8 27.4 %collective-permute-start.4 = (bf16[2048,256]{1,0:T(8,128)(2,1)}, bf16[2048,256]{1,0:T(8,128)(2,1)}, u32[]{:S(2)}, u32[]{:S(2)}) collective-permute-start(bf16[2048,256]{1,0:T(8,128)(2,1)} %shard_map.64.refs_1_.refs_3_), channel_id=1, source_target_pairs={{4,8},{8,4},{5,9},{9,5},{6,10},{10,6},{7,11},{11,7},{20,24},{24,20... | collective-permute-start | bytes 3145736 | tf_op jit(solution)/shard_map/ppermute | solution.py:499
  56.2 34.3 %collective-permute-start.7 = (bf16[2048,256]{1,0:T(8,128)(2,1)}, bf16[2048,256]{1,0:T(8,128)(2,1)}, u32[]{:S(2)}, u32[]{:S(2)}) collective-permute-start(bf16[2048,256]{1,0:T(8,128)(2,1)} %shard_map.68.refs_4_), channel_id=1, source_target_pairs={{4,0},{8,12},{5,1},{9,13},{6,2},{10,14},{7,3},{11,15},{20,16},{24,... | collective-permute-start | bytes 3145736 | tf_op jit(solution)/shard_map/ppermute | solution.py:499
  62.4 38.7 %collective-permute-start.3 = (bf16[2048,256]{1,0:T(8,128)(2,1)}, bf16[2048,256]{1,0:T(8,128)(2,1)}, u32[]{:S(2)}, u32[]{:S(2)}) collective-permute-start(bf16[2048,256]{1,0:T(8,128)(2,1)} %shard_map.67.refs_3_.refs_7_), channel_id=1, source_target_pairs={{4,8},{8,4},{5,9},{9,5},{6,10},{10,6},{7,11},{11,7},{20,24},{24,20... | collective-permute-start | bytes 3145736 | tf_op jit(solution)/shard_map/ppermute | solution.py:499
  64.6 40.8 %collective-permute-start.11 = (bf16[2048,256]{1,0:T(8,128)(2,1)}, bf16[2048,256]{1,0:T(8,128)(2,1)S(1)}, u32[]{:S(2)}, u32[]{:S(2)}) collective-permute-start(bf16[2048,256]{1,0:T(8,128)(2,1)} %shard_map.69.refs_5_), channel_id=1, source_target_pairs={{4,0},{8,12},{5,1},{9,13},{6,2},{10,14},{7,3},{11,15},{20,16},{24,... | collective-permute-start | bytes 3145736 | tf_op jit(solution)/shard_map/ppermute | solution.py:499
  65.9 24.5 %copy-start.5 = (bf16[2,16,32,256]{3,2,1,0:T(8,128)(2,1)S(1)}, bf16[2,16,32,256]{3,2,1,0:T(8,128)(2,1)}, u32[]{:S(2)}) copy-start(bf16[2,16,32,256]{3,2,1,0:T(8,128)(2,1)} %copy-done.4) | copy-start | bytes 1572868
  99.8 20.7 %collective-permute-start.10 = (bf16[8,32,1024]{2,1,0:T(8,128)(2,1)S(1)}, bf16[8,32,1024]{2,1,0:T(8,128)(2,1)S(1)}, u32[]{:S(2)}, u32[]{:S(2)}) collective-permute-start(bf16[8,32,1024]{2,1,0:T(8,128)(2,1)S(1)} %get-tuple-element.36), channel_id=1, source_target_pairs={{4,0},{8,12},{5,1},{9,13},{6,2},{10,14},{7,3},{11,15},{20,16},{24,... | collective-permute-start | bytes 1572872 | tf_op jit(solution)/shard_map/ppermute | solution.py:499
  102.4 29.7 %collective-permute-start.9 = (bf16[8,32,1024]{2,1,0:T(8,128)(2,1)S(1)}, bf16[8,32,1024]{2,1,0:T(8,128)(2,1)S(1)}, u32[]{:S(2)}, u32[]{:S(2)}) collective-permute-start(bf16[8,32,1024]{2,1,0:T(8,128)(2,1)S(1)} %get-tuple-element.35), channel_id=1, source_target_pairs={{4,0},{8,12},{5,1},{9,13},{6,2},{10,14},{7,3},{11,15},{20,16},{24,... | collective-permute-start | bytes 1572872 | tf_op jit(solution)/shard_map/ppermute | solution.py:499
where the time goes:
time: 136 us; the launch traced here: 134 us
  waiting for transfers between devices  58.7 us (43%)
  Pallas kernels  38.8 us (29%)
  starting transfers between devices  28.8 us (21%)
  local copies, waits for them, and re-layouts  6.97 us (5%)
    ppermute x12, waiting for transfers between devices, send(): return lax.ppermute(value, 'seq', pairs)  58.7 us
    pallas_call x6, Pallas kernels, attend(): pl.pallas_call(functools.partial(attend_kernel, passes, len(cands), per_k...  29 us
    ppermute x12, starting transfers between devices, send(): return lax.ppermute(value, 'seq', pairs)  28.8 us
    transpose x1, local copies, waits for them, and re-layouts, two_heads(): return lambda pairs: jnp.transpose(pairs[:, start:start + 2], (1, 0, 2))  3.64 us
    pallas_call x2, Pallas kernels, merge(): pl.pallas_call(functools.partial(merge_kernel, target, head), out_shape=j...  3.03 us
    pallas_call x1, Pallas kernels, cut(): pl.pallas_call(cut_kernel, out_shape=[shape, shape], in_specs=[HBM], out_...  2.9 us
  transfers between devices with their start and end apart: 12, of which 7 were waited for; matrix products, arithmetic and copies ran while one was open for 0% of the time, Pallas kernels for 28%

commit v1 on v0

--- a/solution.py
+++ b/solution.py
@@ -22,7 +22,7 @@
 TN = (((0,), (0,)), ((), ()))
 BLOCK = 512
 SCORE_BLOCK = 1024
-CHUNK = 32
+CHUNK = 64
 GROUPS = 12
 
 

time: 136 us -> 138 us (1.015)
  the two profiles are of different devices: /device:TPU:4 before, /device:TPU:0 now
where the time goes in v1:
time: 138 us; the launch traced here: 136 us
  waiting for transfers between devices  62.1 us (45%)
  Pallas kernels  37.3 us (27%)
  starting transfers between devices  29.1 us (21%)
  local copies, waits for them, and re-layouts  6.97 us (5%)
    ppermute x12, waiting for transfers between devices, send(): return lax.ppermute(value, 'seq', pairs)  62.1 us
    ppermute x12, starting transfers between devices, send(): return lax.ppermute(value, 'seq', pairs)  29.1 us
    pallas_call x6, Pallas kernels, attend(): pl.pallas_call(functools.partial(attend_kernel, passes, len(cands), per_k...  27.6 us
    transpose x1, local copies, waits for them, and re-layouts, two_heads(): return lambda pairs: jnp.transpose(pairs[:, start:start + 2], (1, 0, 2))  3.64 us
    pallas_call x2, Pallas kernels, merge(): pl.pallas_call(functools.partial(merge_kernel, target, head), out_shape=j...  2.96 us
    pallas_call x1, Pallas kernels, cut(): pl.pallas_call(cut_kernel, out_shape=[shape, shape], in_specs=[HBM], out_...  2.9 us
  transfers between devices with their start and end apart: 12, of which 6 were waited for; matrix products, arithmetic and copies ran while one was open for 0% of the time, Pallas kernels for 26%

profile of v1, /device:TPU:0, one launch (start us, length us, event | category | flops | bytes accessed | tf_op | source)
XLA Modules:
  0.0 136.0 jit_solution(5958411706037994545)
XLA Ops:
  0.0 5.2 %conditional.3 = (bf16[2,2048,256]{2,1,0:T(8,128)(2,1)}) conditional(s32[]{:T(128)} %clamp.4, bf16[2048,4,256]{2,1,0:T(4,128)(2,1)} %bitcast.17, bf16[2048,4,256]{2,1,0:T(4,128)(2,1)} %bitcast.18), branch_computations={%region_2.3_spmd, %region_3.4_spmd} | conditional | bytes 8388616 | solution.py:508
  0.0 3.6 %slice_bitcast_fusion.2 = bf16[2,2048,256]{2,0,1:T(2,128)(2,1)S(1)} fusion(bf16[2048,4,256]{2,1,0:T(4,128)(2,1)} %param.2), kind=kLoop, calls=%fused_computation.2 | loop fusion | bytes 4194304 | tf_op jit(solution)/shard_map/cond/branch_0_fun/transpose | solution.py:502
  3.7 1.6 %copy.30 = bf16[2,2048,256]{2,1,0:T(8,128)(2,1)} copy(bf16[2,2048,256]{2,0,1:T(2,128)(2,1)S(1)} %slice_bitcast_fusion.2) | data formatting | bytes 4194304 | tf_op jit(solution)/shard_map/cond | solution.py:508
  5.2 1.4 %collective-permute-start.6 = (bf16[2,2048,256]{2,1,0:T(8,128)(2,1)}, bf16[2,2048,256]{2,1,0:T(8,128)(2,1)}, u32[]{:S(2)}, u32[]{:S(2)}) collective-permute-start(bf16[2,2048,256]{2,1,0:T(8,128)(2,1)} %get-tuple-element.40.pair.refs_3_), channel_id=1, source_target_pairs={{4,0},{8,12},{5,1},{9,13},{6,2},{10,14},{7,3},{11,15},{20,16},{24,... | collective-permute-start | bytes 6291464 | tf_op jit(solution)/shard_map/ppermute | solution.py:499
  6.6 2.9 %shard_map.62 = (bf16[2048,256]{1,0:T(8,128)(2,1)}, bf16[2048,256]{1,0:T(8,128)(2,1)}) custom-call(bf16[2,2048,256]{2,1,0:T(8,128)(2,1)} %get-tuple-element.40.pair.refs_3_), custom_call_target="tpu_custom_call" | custom-call | tf_op jit(solution)/shard_map/pallas_call | solution.py:431
  9.6 7.2 %collective-permute-start = (bf16[2048,256]{1,0:T(8,128)(2,1)}, bf16[2048,256]{1,0:T(8,128)(2,1)}, u32[]{:S(2)}, u32[]{:S(2)}) collective-permute-start(bf16[2048,256]{1,0:T(8,128)(2,1)} %get-tuple-element.27), channel_id=1, source_target_pairs={{0,4},{12,8},{1,5},{13,9},{2,6},{14,10},{3,7},{15,11},{16,20},{28,... | collective-permute-start | bytes 3145736 | tf_op jit(solution)/shard_map/ppermute | solution.py:499
  16.8 1.6 %collective-permute-start.5 = (bf16[2048,256]{1,0:T(8,128)(2,1)}, bf16[2048,256]{1,0:T(8,128)(2,1)}, u32[]{:S(2)}, u32[]{:S(2)}) collective-permute-start(bf16[2048,256]{1,0:T(8,128)(2,1)} %get-tuple-element.27), channel_id=1, source_target_pairs={{4,8},{8,4},{5,9},{9,5},{6,10},{10,6},{7,11},{11,7},{20,24},{24,20... | collective-permute-start | bytes 3145736 | tf_op jit(solution)/shard_map/ppermute | solution.py:499
  18.4 5.4 %collective-permute-start.2 = (bf16[2048,256]{1,0:T(8,128)(2,1)}, bf16[2048,256]{1,0:T(8,128)(2,1)}, u32[]{:S(2)}, u32[]{:S(2)}) collective-permute-start(bf16[2048,256]{1,0:T(8,128)(2,1)} %get-tuple-element.29), channel_id=1, source_target_pairs={{0,4},{12,8},{1,5},{13,9},{2,6},{14,10},{3,7},{15,11},{16,20},{28,... | collective-permute-start | bytes 3145736 | tf_op jit(solution)/shard_map/ppermute | solution.py:499
  23.8 1.6 %collective-permute-start.8 = (bf16[2048,256]{1,0:T(8,128)(2,1)}, bf16[2048,256]{1,0:T(8,128)(2,1)}, u32[]{:S(2)}, u32[]{:S(2)}) collective-permute-start(bf16[2048,256]{1,0:T(8,128)(2,1)} %get-tuple-element.29), channel_id=1, source_target_pairs={{4,8},{8,4},{5,9},{9,5},{6,10},{10,6},{7,11},{11,7},{20,24},{24,20... | collective-permute-start | bytes 3145736 | tf_op jit(solution)/shard_map/ppermute | solution.py:499
  25.5 0.5 conditional.2
  25.5 0.4 slice_bitcast_fusion
  25.9 0.1 copy.28
  26.0 0.1 copy-done.2
  26.1 0.0 copy-done.3
  26.1 0.1 concatenate.3.facts.refs_0_
  26.2 1.0 copy-done
  27.3 1.4 shard_map.61.refs_4_.refs_0_
  28.7 12.1 %shard_map.63 = (bf16[16,32,2048]{2,1,0:T(8,128)(2,1)}, s32[1]{0:T(128)}) custom-call(s32[44]{0:T(128)S(1)} %concatenate.3.facts.refs_0_, bf16[16,32,2048]{2,1,0:T(8,128)(2,1)S(1)} %copy-done, bf16[2,16,32,256]{3,2,1,0:T(8,128)(2,1)S(1)} %get-tuple-element.39.own_ref.refs_2_.refs_3_, bf16[2,2048,256]{2,1,0:T(8,128)(2,1)} %get-tuple-element.40.pair.refs_3_, ...), custom_call_target="tpu_custom_call" | custom-call | flops 8388608 | bytes 65536 | tf_op jit(solution)/shard_map/pallas_call | solution.py:331
  40.8 0.0 collective-permute-done.refs_0_
  40.8 0.6 shard_map.64.refs_1_.refs_3_
  41.5 3.3 %collective-permute-start.1 = (bf16[8,32,2688]{2,1,0:T(8,128)(2,1)}, bf16[8,32,2688]{2,1,0:T(8,128)(2,1)S(1)}, u32[]{:S(2)}, u32[]{:S(2)}) collective-permute-start(bf16[8,32,2688]{2,1,0:T(8,128)(2,1)} %shard_map.65), channel_id=1, source_target_pairs={{0,4},{12,8},{1,5},{13,9},{2,6},{14,10},{3,7},{15,11},{16,20},{28,... | collective-permute-start | bytes 4128776 | tf_op jit(solution)/shard_map/ppermute | solution.py:499
  44.7 1.3 shard_map.66
  46.1 0.0 collective-permute-done.5.refs_0_
  46.1 1.7 %collective-permute-start.4 = (bf16[2048,256]{1,0:T(8,128)(2,1)}, bf16[2048,256]{1,0:T(8,128)(2,1)}, u32[]{:S(2)}, u32[]{:S(2)}) collective-permute-start(bf16[2048,256]{1,0:T(8,128)(2,1)} %shard_map.64.refs_1_.refs_3_), channel_id=1, source_target_pairs={{4,8},{8,4},{5,9},{9,5},{6,10},{10,6},{7,11},{11,7},{20,24},{24,20... | collective-permute-start | bytes 3145736 | tf_op jit(solution)/shard_map/ppermute | solution.py:499
  47.8 8.4 %collective-permute-done.6.refs_2_.refs_6_ = bf16[2,2048,256]{2,1,0:T(8,128)(2,1)} collective-permute-done((bf16[2,2048,256]{2,1,0:T(8,128)(2,1)}, bf16[2,2048,256]{2,1,0:T(8,128)(2,1)}, u32[]{:S(2)}, u32[]{:S(2)}) %collective-permute-start.6) | collective-permute-done | bytes 2097184 | tf_op jit(solution)/shard_map/ppermute | solution.py:499
  56.2 0.6 shard_map.68.refs_4_
  56.8 1.3 collective-permute-start.7
  58.1 4.0 %collective-permute-done.2.refs_0_ = bf16[2048,256]{1,0:T(8,128)(2,1)} collective-permute-done((bf16[2048,256]{1,0:T(8,128)(2,1)}, bf16[2048,256]{1,0:T(8,128)(2,1)}, u32[]{:S(2)}, u32[]{:S(2)}) %collective-permute-start.2) | collective-permute-done | bytes 1048608 | tf_op jit(solution)/shard_map/ppermute | solution.py:499
  62.1 0.6 shard_map.67.refs_3_.refs_7_
  62.7 1.6 %collective-permute-start.3 = (bf16[2048,256]{1,0:T(8,128)(2,1)}, bf16[2048,256]{1,0:T(8,128)(2,1)}, u32[]{:S(2)}, u32[]{:S(2)}) collective-permute-start(bf16[2048,256]{1,0:T(8,128)(2,1)} %shard_map.67.refs_3_.refs_7_), channel_id=1, source_target_pairs={{4,8},{8,4},{5,9},{9,5},{6,10},{10,6},{7,11},{11,7},{20,24},{24,20... | collective-permute-start | bytes 3145736 | tf_op jit(solution)/shard_map/ppermute | solution.py:499
  64.3 0.0 collective-permute-done.8.refs_0_
  64.3 0.6 shard_map.69.refs_5_
  65.0 1.3 collective-permute-start.11
  66.3 2.1 %shard_map.70 = (bf16[16,32,2048]{2,1,0:T(8,128)(2,1)}, s32[1]{0:T(128)}) custom-call(s32[44]{0:T(128)S(1)} %concatenate.3.facts.refs_0_, bf16[16,32,2048]{2,1,0:T(8,128)(2,1)S(1)} %copy-done, bf16[2,16,32,256]{3,2,1,0:T(8,128)(2,1)} %copy-done.4, bf16[2048,256]{1,0:T(8,128)(2,1)} %shard_map.67.refs_3_.refs_7_, ...), custom_call_target="tpu_custom_call", output_to_operand_aliasing={{0}: (8, {})} | custom-call | flops 16777216 | bytes 65536 | tf_op jit(solution)/shard_map/pallas_call | solution.py:331
  68.4 0.0 collective-permute-done.4.refs_4_
  68.4 22.7 %collective-permute-done.1.refs_1_ = bf16[8,32,2688]{2,1,0:T(8,128)(2,1)S(1)} collective-permute-done((bf16[8,32,2688]{2,1,0:T(8,128)(2,1)}, bf16[8,32,2688]{2,1,0:T(8,128)(2,1)S(1)}, u32[]{:S(2)}, u32[]{:S(2)}) %collective-permute-start.1) | collective-permute-done | bytes 1376288 | tf_op jit(solution)/shard_map/ppermute | solution.py:499
  91.1 0.0 collective-permute-done.7.refs_5_
  91.1 5.8 %shard_map.71 = (bf16[16,32,2048]{2,1,0:T(8,128)(2,1)}, bf16[8,32,1024]{2,1,0:T(8,128)(2,1)S(1)}, s32[1]{0:T(128)}) custom-call(s32[44]{0:T(128)S(1)} %concatenate.3.facts.refs_0_, bf16[8,32,2688]{2,1,0:T(8,128)(2,1)S(1)} %collective-permute-done.1.refs_1_, bf16[16,32,2048]{2,1,0:T(8,128)(2,1)S(1)} %copy-done, ...), custom_call_target="tpu_custom_call", output_to_operand_aliasing={{0}: (6, {})} | custom-call | flops 8388608 | bytes 65536 | tf_op jit(solution)/shard_map/pallas_call | solution.py:331
  96.9 1.3 collective-permute-start.10
  98.2 0.0 collective-permute-done.3.refs_4_.refs_3_
  98.2 1.3 shard_map.72
  99.5 1.3 collective-permute-start.9
  100.8 6.6 %collective-permute-done.11.refs_4_ = bf16[2048,256]{1,0:T(8,128)(2,1)S(1)} collective-permute-done((bf16[2048,256]{1,0:T(8,128)(2,1)}, bf16[2048,256]{1,0:T(8,128)(2,1)S(1)}, u32[]{:S(2)}, u32[]{:S(2)}) %collective-permute-start.11) | collective-permute-done | bytes 1048608 | tf_op jit(solution)/shard_map/ppermute | solution.py:499
  107.4 4.9 %shard_map.73 = (bf16[16,32,2048]{2,1,0:T(8,128)(2,1)}, s32[1]{0:T(128)}) custom-call(s32[44]{0:T(128)S(1)} %concatenate.3.facts.refs_0_, bf16[16,32,2048]{2,1,0:T(8,128)(2,1)S(1)} %copy-done, bf16[2,16,32,256]{3,2,1,0:T(8,128)(2,1)S(1)} %copy-done.5, bf16[2048,256]{1,0:T(8,128)(2,1)} %collective-permute-done.3.refs_4_.refs_3_, ...), custom_call_target="tpu_custom_call", output_to_operand_aliasing={{0}: (5, {})} | custom-call | flops 4194304 | bytes 65536 | tf_op jit(solution)/shard_map/pallas_call | solution.py:331
  112.4 5.2 %collective-permute-done.10.got = bf16[8,32,1024]{2,1,0:T(8,128)(2,1)S(1)} collective-permute-done((bf16[8,32,1024]{2,1,0:T(8,128)(2,1)S(1)}, bf16[8,32,1024]{2,1,0:T(8,128)(2,1)S(1)}, u32[]{:S(2)}, u32[]{:S(2)}) %collective-permute-start.10) | collective-permute-done | bytes 524320 | tf_op jit(solution)/shard_map/ppermute | solution.py:499
  117.5 1.5 %shard_map.74.old = bf16[16,32,2048]{2,1,0:T(8,128)(2,1)} custom-call(s32[44]{0:T(128)S(1)} %concatenate.3.facts.refs_0_, s32[16]{0:T(128)S(1)} %copy-done.2, s32[16]{0:T(128)S(1)} %copy-done.3, bf16[8,32,1024]{2,1,0:T(8,128)(2,1)S(1)} %collective-permute-done.10.got, bf16[16,32,2048]{2,1,0:T(8,128)(2,1)} %get-tuple-element.38.old), custom_call_target="tpu_custom_call", output_to_operand_aliasing={{}: (4, {})} | custom-call | tf_op jit(solution)/shard_map/pallas_call | solution.py:467
  119.0 15.3 %collective-permute-done.9.got = bf16[8,32,1024]{2,1,0:T(8,128)(2,1)S(1)} collective-permute-done((bf16[8,32,1024]{2,1,0:T(8,128)(2,1)S(1)}, bf16[8,32,1024]{2,1,0:T(8,128)(2,1)S(1)}, u32[]{:S(2)}, u32[]{:S(2)}) %collective-permute-start.9) | collective-permute-done | bytes 524320 | tf_op jit(solution)/shard_map/ppermute | solution.py:499
  134.3 1.5 %shard_map.75 = bf16[16,32,2048]{2,1,0:T(8,128)(2,1)} custom-call(s32[44]{0:T(128)S(1)} %concatenate.3.facts.refs_0_, s32[16]{0:T(128)S(1)} %copy-done.2, s32[16]{0:T(128)S(1)} %copy-done.3, bf16[8,32,1024]{2,1,0:T(8,128)(2,1)S(1)} %collective-permute-done.9.got, bf16[16,32,2048]{2,1,0:T(8,128)(2,1)} %shard_map.74.old), custom_call_target="tpu_custom_call", output_to_operand_aliasing={{}: (4, {})} | custom-call | tf_op jit(solution)/shard_map/pallas_call | solution.py:467
  (12 shorter events, 0.0 us)
Async XLA Ops:
  5.2 20.3 %copy-start.6 = (bf16[16,32,4,256]{3,2,1,0:T(4,128)(2,1)S(1)}, bf16[16,32,4,256]{3,2,1,0:T(4,128)(2,1)}, u32[]{:S(2)}) copy-start(bf16[16,32,4,256]{3,2,1,0:T(4,128)(2,1)} %param.10) | copy-start | bytes 3145732
  5.2 51.0 %collective-permute-start.6 = (bf16[2,2048,256]{2,1,0:T(8,128)(2,1)}, bf16[2,2048,256]{2,1,0:T(8,128)(2,1)}, u32[]{:S(2)}, u32[]{:S(2)}) collective-permute-start(bf16[2,2048,256]{2,1,0:T(8,128)(2,1)} %get-tuple-element.40.pair.refs_3_), channel_id=1, source_target_pairs={{4,0},{8,12},{5,1},{9,13},{6,2},{10,14},{7,3},{11,15},{20,16},{24,... | collective-permute-start | bytes 6291464 | tf_op jit(solution)/shard_map/ppermute | solution.py:499
  9.6 31.2 %collective-permute-start = (bf16[2048,256]{1,0:T(8,128)(2,1)}, bf16[2048,256]{1,0:T(8,128)(2,1)}, u32[]{:S(2)}, u32[]{:S(2)}) collective-permute-start(bf16[2048,256]{1,0:T(8,128)(2,1)} %get-tuple-element.27), channel_id=1, source_target_pairs={{0,4},{12,8},{1,5},{13,9},{2,6},{14,10},{3,7},{15,11},{16,20},{28,... | collective-permute-start | bytes 3145736 | tf_op jit(solution)/shard_map/ppermute | solution.py:499
  16.8 29.3 %collective-permute-start.5 = (bf16[2048,256]{1,0:T(8,128)(2,1)}, bf16[2048,256]{1,0:T(8,128)(2,1)}, u32[]{:S(2)}, u32[]{:S(2)}) collective-permute-start(bf16[2048,256]{1,0:T(8,128)(2,1)} %get-tuple-element.27), channel_id=1, source_target_pairs={{4,8},{8,4},{5,9},{9,5},{6,10},{10,6},{7,11},{11,7},{20,24},{24,20... | collective-permute-start | bytes 3145736 | tf_op jit(solution)/shard_map/ppermute | solution.py:499
  18.4 43.7 %collective-permute-start.2 = (bf16[2048,256]{1,0:T(8,128)(2,1)}, bf16[2048,256]{1,0:T(8,128)(2,1)}, u32[]{:S(2)}, u32[]{:S(2)}) collective-permute-start(bf16[2048,256]{1,0:T(8,128)(2,1)} %get-tuple-element.29), channel_id=1, source_target_pairs={{0,4},{12,8},{1,5},{13,9},{2,6},{14,10},{3,7},{15,11},{16,20},{28,... | collective-permute-start | bytes 3145736 | tf_op jit(solution)/shard_map/ppermute | solution.py:499
  23.8 40.5 %collective-permute-start.8 = (bf16[2048,256]{1,0:T(8,128)(2,1)}, bf16[2048,256]{1,0:T(8,128)(2,1)}, u32[]{:S(2)}, u32[]{:S(2)}) collective-permute-start(bf16[2048,256]{1,0:T(8,128)(2,1)} %get-tuple-element.29), channel_id=1, source_target_pairs={{4,8},{8,4},{5,9},{9,5},{6,10},{10,6},{7,11},{11,7},{20,24},{24,20... | collective-permute-start | bytes 3145736 | tf_op jit(solution)/shard_map/ppermute | solution.py:499
  25.5 0.7 copy-start.2
  25.5 0.7 copy-start.3
  25.5 1.8 %copy-start = (bf16[16,32,2048]{2,1,0:T(8,128)(2,1)S(1)}, bf16[16,32,2048]{2,1,0:T(8,128)(2,1)}, u32[]{:S(2)}) copy-start(bf16[16,32,2048]{2,1,0:T(8,128)(2,1)} %refs_1_.7) | copy-start | bytes 6291460
  26.0 15.4 %copy-start.4 = (bf16[2,16,32,256]{3,2,1,0:T(8,128)(2,1)}, bf16[2,16,32,256]{3,2,1,0:T(8,128)(2,1)S(1)}, u32[]{:S(2)}) copy-start(bf16[2,16,32,256]{3,2,1,0:T(8,128)(2,1)S(1)} %get-tuple-element.39.own_ref.refs_2_.refs_3_) | copy-start | bytes 1572868
  28.7 12.1 %copy-start.1 = (bf16[8,32,2688]{2,1,0:T(8,128)(2,1)}, bf16[8,32,2688]{2,1,0:T(8,128)(2,1)S(1)}, u32[]{:S(2)}) copy-start(bf16[8,32,2688]{2,1,0:T(8,128)(2,1)S(1)} %shard_map.61.refs_4_.refs_0_) | copy-start | bytes 4128772
  41.5 49.6 %collective-permute-start.1 = (bf16[8,32,2688]{2,1,0:T(8,128)(2,1)}, bf16[8,32,2688]{2,1,0:T(8,128)(2,1)S(1)}, u32[]{:S(2)}, u32[]{:S(2)}) collective-permute-start(bf16[8,32,2688]{2,1,0:T(8,128)(2,1)} %shard_map.65), channel_id=1, source_target_pairs={{0,4},{12,8},{1,5},{13,9},{2,6},{14,10},{3,7},{15,11},{16,20},{28,... | collective-permute-start | bytes 4128776 | tf_op jit(solution)/shard_map/ppermute | solution.py:499
  46.1 22.3 %collective-permute-start.4 = (bf16[2048,256]{1,0:T(8,128)(2,1)}, bf16[2048,256]{1,0:T(8,128)(2,1)}, u32[]{:S(2)}, u32[]{:S(2)}) collective-permute-start(bf16[2048,256]{1,0:T(8,128)(2,1)} %shard_map.64.refs_1_.refs_3_), channel_id=1, source_target_pairs={{4,8},{8,4},{5,9},{9,5},{6,10},{10,6},{7,11},{11,7},{20,24},{24,20... | collective-permute-start | bytes 3145736 | tf_op jit(solution)/shard_map/ppermute | solution.py:499
  56.8 34.3 %collective-permute-start.7 = (bf16[2048,256]{1,0:T(8,128)(2,1)}, bf16[2048,256]{1,0:T(8,128)(2,1)}, u32[]{:S(2)}, u32[]{:S(2)}) collective-permute-start(bf16[2048,256]{1,0:T(8,128)(2,1)} %shard_map.68.refs_4_), channel_id=1, source_target_pairs={{4,0},{8,12},{5,1},{9,13},{6,2},{10,14},{7,3},{11,15},{20,16},{24,... | collective-permute-start | bytes 3145736 | tf_op jit(solution)/shard_map/ppermute | solution.py:499
  62.7 35.5 %collective-permute-start.3 = (bf16[2048,256]{1,0:T(8,128)(2,1)}, bf16[2048,256]{1,0:T(8,128)(2,1)}, u32[]{:S(2)}, u32[]{:S(2)}) collective-permute-start(bf16[2048,256]{1,0:T(8,128)(2,1)} %shard_map.67.refs_3_.refs_7_), channel_id=1, source_target_pairs={{4,8},{8,4},{5,9},{9,5},{6,10},{10,6},{7,11},{11,7},{20,24},{24,20... | collective-permute-start | bytes 3145736 | tf_op jit(solution)/shard_map/ppermute | solution.py:499
  65.0 42.5 %collective-permute-start.11 = (bf16[2048,256]{1,0:T(8,128)(2,1)}, bf16[2048,256]{1,0:T(8,128)(2,1)S(1)}, u32[]{:S(2)}, u32[]{:S(2)}) collective-permute-start(bf16[2048,256]{1,0:T(8,128)(2,1)} %shard_map.69.refs_5_), channel_id=1, source_target_pairs={{4,0},{8,12},{5,1},{9,13},{6,2},{10,14},{7,3},{11,15},{20,16},{24,... | collective-permute-start | bytes 3145736 | tf_op jit(solution)/shard_map/ppermute | solution.py:499
  66.3 24.8 %copy-start.5 = (bf16[2,16,32,256]{3,2,1,0:T(8,128)(2,1)S(1)}, bf16[2,16,32,256]{3,2,1,0:T(8,128)(2,1)}, u32[]{:S(2)}) copy-start(bf16[2,16,32,256]{3,2,1,0:T(8,128)(2,1)} %copy-done.4) | copy-start | bytes 1572868
  96.9 20.6 %collective-permute-start.10 = (bf16[8,32,1024]{2,1,0:T(8,128)(2,1)S(1)}, bf16[8,32,1024]{2,1,0:T(8,128)(2,1)S(1)}, u32[]{:S(2)}, u32[]{:S(2)}) collective-permute-start(bf16[8,32,1024]{2,1,0:T(8,128)(2,1)S(1)} %get-tuple-element.36), channel_id=1, source_target_pairs={{4,0},{8,12},{5,1},{9,13},{6,2},{10,14},{7,3},{11,15},{20,16},{24,... | collective-permute-start | bytes 1572872 | tf_op jit(solution)/shard_map/ppermute | solution.py:499
  99.5 34.8 %collective-permute-start.9 = (bf16[8,32,1024]{2,1,0:T(8,128)(2,1)S(1)}, bf16[8,32,1024]{2,1,0:T(8,128)(2,1)S(1)}, u32[]{:S(2)}, u32[]{:S(2)}) collective-permute-start(bf16[8,32,1024]{2,1,0:T(8,128)(2,1)S(1)} %get-tuple-element.35), channel_id=1, source_target_pairs={{4,0},{8,12},{5,1},{9,13},{6,2},{10,14},{7,3},{11,15},{20,16},{24,... | collective-permute-start | bytes 1572872 | tf_op jit(solution)/shard_map/ppermute | solution.py:499
